TPU v7x, 128 devices: a whole 4x4x4 slice. The times are simulated.
128 devices in a mesh: section: 2 (over core), tp: 64 (over z, y, x).
Axes of the slice: x: 4, y: 4, z: 4, core: 2. Of those that a mesh axis runs over, the one named last changes fastest.
Arguments:
- incoming_hidden_states: bfloat16 [16, 8192], replicated, may hold values from -6 to 6
- parent_positions: int32 [16], replicated, may hold values from 0 to 15
- filled_extents: int32 [16], replicated, may hold values from 1 to 32, as said below
- stored_address_tensor: bfloat16 [2, 16, 32, 1024], P('section'), may hold values from -6 to 6
- stored_content_tensor: bfloat16 [2, 16, 32, 1024], P('section'), may hold values from -6 to 6
- layer_scale_factors: bfloat16 [2, 8192], P('section'), may hold values from 0.5 to 1.5
- question_matrix: bfloat16 [2, 8192, 8192], P('section', None, 'tp'), may hold values from -0.0625 to 0.0625
- address_content_matrix: bfloat16 [2, 8192, 2048], P('section'), may hold values from -0.0625 to 0.0625
- projection_back_matrix: bfloat16 [2, 8192, 8192], P('section', 'tp'), may hold values from -0.0625 to 0.0625
- ending_scale_factors: bfloat16 [8192], replicated, may hold values from 0.5 to 1.5
- lexicon_matrix: bfloat16 [32768, 8192], P(('section', 'tp')), may hold values from -0.1875 to 0.1875
- sampling_warmth: float32 [16], replicated, may hold values from 0.6 to 1.4
- sampling_noise: float32 [16, 32768], P(None, ('section', 'tp')), as said below
Outputs:
- new_entries: bfloat16 [2, 16, 2048], P('section', None, 'tp')
- final_hidden: bfloat16 [16, 8192], replicated
- top_score: float32 [16], replicated
- log_norm: float32 [16], replicated
Inputs may be any that keep to these rules, and one draw needn't show every extreme that they name: Slot j continues old slot parent_positions[j]; an old slot may be named several times or not at all. `filled_extents`: some old slot has exactly 32 filled slots and some exactly one. `sampling_noise`: standard Gumbel noise.
All inputs are finite; a program needn't handle non-finite values.
Results may differ from a plain program's by a relative error of at most 0.013.
Values may be sent and summed in bfloat16 or wider, within the bound.
No kernel may reach another device: no remote copies, remote signals or barrier semaphores. Data moves between devices by JAX's collectives and lax.ppermute only.
A program may use at most 128 MiB of HBM per device.

v0:
```python
import functools

import jax
import jax.numpy as jnp
from jax import lax
from jax.experimental import pallas as pl
from jax.experimental.pallas import tpu as pltpu
from jax.sharding import PartitionSpec as P

HEAD = 128
KV_HEADS = 8
STEPS = 4
LIMIT = 16 * 1024 * 1024


epsilon = 1e-05


def dot(a, b, contract=((1,), (0,))):
    return lax.dot_general(a, b, (contract, ((), ())), preferred_element_type=jnp.float32)


def weights_of(width, pieces):
    step = width // pieces
    return [(i * step, step) for i in range(pieces)]


def column_of(scalars, rows):
    row = lax.broadcasted_iota(jnp.int32, (rows, HEAD), 0)
    column = jnp.zeros((rows, HEAD), scalars[0].dtype)
    for j in range(rows):
        column = jnp.where(row == j, scalars[j], column)
    return column


def attend(query, pair, keys, values, visible_slots):
    rows = query.shape[0]
    slots = keys.shape[0] // rows
    new_key = pair[:, :HEAD].astype(jnp.float32)
    new_value = pair[:, HEAD:].astype(jnp.float32)
    score_scale = HEAD ** (-0.5)
    row = lax.broadcasted_iota(jnp.int32, (rows, rows * slots), 0)
    column = lax.broadcasted_iota(jnp.int32, (rows, rows * slots), 1)
    slot = column - row * slots
    visible = (slot >= 0) & (slot < visible_slots[:, :1])
    scores = dot(query, keys, ((1,), (1,))) * score_scale
    own_score = jnp.sum(query.astype(jnp.float32) * new_key, axis=1, keepdims=True) * score_scale
    highest = jnp.maximum(
        jnp.max(jnp.where(visible, scores, -1e30), axis=1, keepdims=True), own_score
    )
    spread = jnp.where(visible, jnp.exp(scores - highest), 0.0)
    own_weight = jnp.exp(own_score - highest)
    denominator = jnp.sum(spread, axis=1, keepdims=True) + own_weight
    probabilities = (spread / denominator).astype(jnp.bfloat16)
    own_prob = (own_weight / denominator).astype(jnp.bfloat16).astype(jnp.float32)
    mixed = dot(probabilities, values) + own_prob * new_value
    return mixed.astype(jnp.bfloat16)


def store_terms(mixed, back, terms_ref):
    terms = dot(mixed, back)
    rows = terms_ref.shape[1]
    parts = mixed.shape[0] // rows
    shards = terms_ref.shape[0] // parts
    for k in range(back.shape[1] // HEAD):
        for p in range(parts):
            block = terms[p * rows : (p + 1) * rows, k * HEAD : (k + 1) * HEAD]
            terms_ref[p * shards + k] = block.astype(jnp.bfloat16)


def lane_squares(hidden):
    total = hidden[:, :HEAD] * hidden[:, :HEAD]
    for k in range(HEAD, hidden.shape[1], HEAD):
        total = total + hidden[:, k : k + HEAD] * hidden[:, k : k + HEAD]
    return total


def share_of(block, own_ref):
    rows = own_ref.shape[0]
    own = block[:rows]
    for p in range(1, block.shape[0] // rows):
        own = jnp.where(lax.axis_index("section") == p, block[p * rows : (p + 1) * rows], own)
    own_ref[...] = own


def whole_rows(blocks_ref, shards, k):
    parts = [blocks_ref[i + k].astype(jnp.float32) for i in range(0, blocks_ref.shape[0], shards)]
    return jnp.concatenate(parts, axis=0)


def first_layer_kernel(
    parents_hbm,
    extents_hbm,
    hidden_hbm,
    gain_hbm,
    question_hbm,
    pair_hbm,
    back_hbm,
    address_hbm,
    content_hbm,
    terms_ref,
    entry_ref,
    own_ref,
    gain_ref,
    question_ref,
    pair_ref,
    back_ref,
    keys_ref,
    values_ref,
    visible_ref,
    parents,
    extents,
    hidden_ref,
    address_ref,
    content_ref,
    sems,
    question_sems,
    pair_sems,
):
    rows, width = hidden_ref.shape
    slots = address_ref.shape[1]
    shard = lax.axis_index("tp")
    group = shard // (lax.axis_size("tp") // KV_HEADS)
    head_columns = pl.ds(pl.multiple_of(group * HEAD, HEAD), HEAD)
    pair_columns = pl.ds(pl.multiple_of(group * 2 * HEAD, 2 * HEAD), 2 * HEAD)
    small = [
        pltpu.make_async_copy(hidden_hbm, hidden_ref, sems.at[0]),
        pltpu.make_async_copy(gain_hbm, gain_ref, sems.at[1]),
        pltpu.make_async_copy(parents_hbm, parents, sems.at[4]),
        pltpu.make_async_copy(extents_hbm, extents, sems.at[5]),
    ]
    lines = [
        pltpu.make_async_copy(address_hbm.at[0, :, :, head_columns], address_ref, sems.at[2]),
        pltpu.make_async_copy(content_hbm.at[0, :, :, head_columns], content_ref, sems.at[3]),
    ]
    projections = []
    for i, (start, step) in enumerate(weights_of(width, STEPS)):
        part = pl.ds(start, step)
        projections.append(
            (
                pltpu.make_async_copy(question_hbm.at[0, part], question_ref.at[part], question_sems.at[i]),
                pltpu.make_async_copy(pair_hbm.at[0, part, pair_columns], pair_ref.at[part], pair_sems.at[i]),
            )
        )
    back = pltpu.make_async_copy(back_hbm.at[0], back_ref, sems.at[6])
    for copy in small:
        copy.start()
    for i, two in enumerate(projections):
        for copy in two:
            copy.start()
        if i == 0:
            for copy in lines:
                copy.start()
    back.start()

    for copy in small:
        copy.wait()
    own = hidden_ref[:, pl.ds(pl.multiple_of(shard * HEAD, HEAD), HEAD)]
    share_of(own.astype(jnp.float32), own_ref)
    squares = jnp.zeros((rows, HEAD), jnp.float32)
    query = jnp.zeros((rows, HEAD), jnp.float32)
    pair = jnp.zeros((rows, 2 * HEAD), jnp.float32)
    for i, (start, step) in enumerate(weights_of(width, STEPS)):
        part = slice(start, start + step)
        hidden = hidden_ref[:, part].astype(jnp.float32)
        squares = squares + lane_squares(hidden)
        scaled = (hidden * gain_ref[:, part].astype(jnp.float32)).astype(jnp.bfloat16)
        if i == STEPS // 2:
            visible = column_of([extents[parents[j]] for j in range(rows)], rows)
            visible_ref[...] = visible
            for copy in lines:
                copy.wait()
            for j in range(rows):
                lines_j = pl.ds(j * slots, slots)
                keys_ref[lines_j] = address_ref[parents[j]]
                values_ref[lines_j] = content_ref[parents[j]]
        for copy in projections[i]:
            copy.wait()
        query = query + dot(scaled, question_ref[part])
        pair = pair + dot(scaled, pair_ref[part])
    squares = jnp.sum(squares, axis=1, keepdims=True)
    inverse = lax.rsqrt(squares * (1.0 / width) + epsilon)
    query = (query * inverse).astype(jnp.bfloat16)
    pair = (pair * inverse).astype(jnp.bfloat16)
    entry_ref[...] = pair
    mixed = attend(query, pair, keys_ref[...], values_ref[...], visible)
    back.wait()
    store_terms(mixed, back_ref[...], terms_ref)


def next_layer_kernel(
    blocks_ref,
    first_ref,
    gain_ref,
    question_ref,
    pair_ref,
    back_ref,
    keys_ref,
    values_ref,
    visible_ref,
    warmth_hbm,
    terms_ref,
    entry_hbm,
    own_ref,
    warmth_ref,
    entry_ref,
    warmth,
    sems,
):
    fetch = pltpu.make_async_copy(warmth_hbm, warmth, sems.at[0])
    fetch.start()
    width = question_ref.shape[0]
    shards = lax.axis_size("tp")
    shard = lax.axis_index("tp")
    rows = first_ref.shape[0]
    share_of(whole_rows(blocks_ref, shards, shard), own_ref)
    hidden = jnp.concatenate([whole_rows(blocks_ref, shards, k) for k in range(shards)], axis=1)
    squares = lane_squares(hidden)
    scaled = (hidden * gain_ref[...].astype(jnp.float32)).astype(jnp.bfloat16)
    query = dot(scaled, question_ref[...])
    pair = dot(scaled, pair_ref[...])
    squares = jnp.sum(squares, axis=1, keepdims=True)
    inverse = lax.rsqrt(squares * (1.0 / width) + epsilon)
    query = (query * inverse).astype(jnp.bfloat16)
    pair = (pair * inverse).astype(jnp.bfloat16)
    both = jnp.where(lax.axis_index("section") == 0, first_ref[...], pair).astype(jnp.float32)
    share = entry_ref.shape[1]
    offset = shard % (shards // KV_HEADS) * share
    both = pltpu.roll(both, 2 * HEAD - offset, 1)
    entry_ref[...] = both[:, :share].astype(jnp.bfloat16)
    leave = pltpu.make_async_copy(entry_ref, entry_hbm, sems.at[1])
    leave.start()
    fetch.wait()
    warmth_ref[...] = column_of([warmth[j] for j in range(rows)], rows)
    mixed = attend(query, pair, keys_ref[...], values_ref[...], visible_ref[...])
    store_terms(mixed, back_ref[...], terms_ref)
    leave.wait()


def in_hbm(*arrays):
    return [pltpu.with_memory_space_constraint(a, pltpu.HBM) for a in arrays]


def specs(kinds):
    spaces = {"s": pltpu.SMEM, "v": pltpu.VMEM, "h": pltpu.HBM}
    return [pl.BlockSpec(memory_space=spaces[kind]) for kind in kinds]


def first_layer(terms_shape, parents, extents, hidden, gain, question, pair, back, address, content):
    rows, width = hidden.shape
    slots = address.shape[2]
    bf16 = functools.partial(jax.ShapeDtypeStruct, dtype=jnp.bfloat16)
    return pl.pallas_call(
        first_layer_kernel,
        out_shape=(
            bf16(terms_shape),
            bf16((rows, 2 * HEAD)),
            jax.ShapeDtypeStruct(terms_shape[1:], jnp.float32),
            bf16((1, width)),
            bf16((width, HEAD)),
            bf16((width, 2 * HEAD)),
            bf16((HEAD, width)),
            bf16((rows * slots, HEAD)),
            bf16((rows * slots, HEAD)),
            jax.ShapeDtypeStruct((rows, HEAD), jnp.int32),
        ),
        in_specs=specs("hhhhhhhhh"),
        out_specs=specs("v" * 10),
        scratch_shapes=[
            pltpu.SMEM((rows,), jnp.int32),
            pltpu.SMEM((rows,), jnp.int32),
            pltpu.VMEM((rows, width), jnp.bfloat16),
            pltpu.VMEM((rows, slots, HEAD), jnp.bfloat16),
            pltpu.VMEM((rows, slots, HEAD), jnp.bfloat16),
            pltpu.SemaphoreType.DMA((7,)),
            pltpu.SemaphoreType.DMA((STEPS,)),
            pltpu.SemaphoreType.DMA((STEPS,)),
        ],
        compiler_params=pltpu.CompilerParams(vmem_limit_bytes=LIMIT),
        name="first_layer",
    )(*in_hbm(parents, extents, hidden, gain, question, pair, back, address, content))


def next_layer(blocks, first, held, warmth, share):
    rows = warmth.shape[0]
    bf16 = functools.partial(jax.ShapeDtypeStruct, dtype=jnp.bfloat16)
    return pl.pallas_call(
        next_layer_kernel,
        out_shape=(
            bf16(blocks.shape),
            bf16((rows, share)),
            jax.ShapeDtypeStruct(blocks.shape[1:], jnp.float32),
            jax.ShapeDtypeStruct((rows, HEAD), jnp.float32),
        ),
        in_specs=specs("v" * (2 + len(held)) + "h"),
        out_specs=specs("vhvv"),
        scratch_shapes=[
            pltpu.VMEM((rows, share), jnp.bfloat16),
            pltpu.SMEM((rows,), jnp.float32),
            pltpu.SemaphoreType.DMA((2,)),
        ],
        compiler_params=pltpu.CompilerParams(vmem_limit_bytes=LIMIT),
        name="next_layer",
    )(blocks, first, *held, *in_hbm(warmth))


def stats_kernel(
    blocks_ref, gain_ref, warmth_ref, noise_ref, lexicon_ref, out_ref, final_hbm, final_ref, sem
):
    rows, width = final_ref.shape
    shards = width // HEAD
    squares = jnp.zeros((rows, HEAD), jnp.float32)
    pieces = []
    for k in range(shards):
        hidden = whole_rows(blocks_ref, shards, k)
        final_ref[:, k * HEAD : (k + 1) * HEAD] = hidden.astype(jnp.bfloat16)
        squares = squares + hidden * hidden
        pieces.append((hidden * gain_ref[k : k + 1].astype(jnp.float32)).astype(jnp.bfloat16))
    leave = pltpu.make_async_copy(final_ref, final_hbm, sem)
    leave.start()
    logits = dot(jnp.concatenate(pieces, axis=1), lexicon_ref[...], ((1,), (1,)))
    squares = jnp.sum(squares, axis=1, keepdims=True)
    inverse = lax.rsqrt(squares * (1.0 / width) + epsilon)
    tempered = logits * inverse / warmth_ref[:, :1]
    best = jnp.max(tempered + noise_ref[...], axis=1, keepdims=True)
    peak = jnp.max(tempered, axis=1, keepdims=True)
    mass = jnp.sum(jnp.exp(tempered - peak), axis=1, keepdims=True)
    norm = peak + jnp.log(mass)
    lane = lax.broadcasted_iota(jnp.int32, (rows, HEAD), 1)
    row = lax.broadcasted_iota(jnp.int32, (rows, HEAD), 0)
    packed = jnp.where(lane == row, best, 0.0)
    packed = jnp.where(lane == row + rows, norm, packed)
    packed = jnp.sum(packed, axis=0, keepdims=True)
    out_ref[...] = jnp.broadcast_to(packed[None], out_ref.shape)
    leave.wait()


def local_stats(blocks, gain, warmth, noise, lexicon):
    rows = warmth.shape[0]
    width = lexicon.shape[1]
    return pl.pallas_call(
        stats_kernel,
        out_shape=(
            jax.ShapeDtypeStruct((blocks.shape[0], 1, HEAD), jnp.float32),
            jax.ShapeDtypeStruct((rows, width), jnp.bfloat16),
        ),
        in_specs=specs("vvvvv"),
        out_specs=tuple(specs("vh")),
        scratch_shapes=[pltpu.VMEM((rows, width), jnp.bfloat16), pltpu.SemaphoreType.DMA],
        compiler_params=pltpu.CompilerParams(vmem_limit_bytes=LIMIT),
        name="local_stats",
    )(blocks, gain, warmth, noise, lexicon)


def combine_kernel(stats_ref, best_hbm, norm_hbm, best_ref, norm_ref, sems):
    rows = best_ref.shape[0]
    stats = stats_ref[...]
    highest = jnp.max(stats, axis=0)
    norm = highest + jnp.log(jnp.sum(jnp.exp(stats - highest[None]), axis=0))
    best_ref[...] = highest[0, :rows]
    norm_ref[...] = norm[0, rows : 2 * rows]
    copies = [
        pltpu.make_async_copy(best_ref, best_hbm, sems.at[0]),
        pltpu.make_async_copy(norm_ref, norm_hbm, sems.at[1]),
    ]
    for copy in copies:
        copy.start()
    for copy in copies:
        copy.wait()


def combine(stats, rows):
    row = jax.ShapeDtypeStruct((rows,), jnp.float32)
    return pl.pallas_call(
        combine_kernel,
        out_shape=(row, row),
        in_specs=specs("v"),
        out_specs=specs("hh"),
        compiler_params=pltpu.CompilerParams(vmem_limit_bytes=LIMIT // 4),
        scratch_shapes=[
            pltpu.VMEM((rows,), jnp.float32),
            pltpu.VMEM((rows,), jnp.float32),
            pltpu.SemaphoreType.DMA((2,)),
        ],
        name="combine",
    )(stats)


def per_device(
    incoming_hidden_states,
    parent_positions,
    filled_extents,
    stored_address_tensor,
    stored_content_tensor,
    layer_scale_factors,
    question_matrix,
    address_content_matrix,
    projection_back_matrix,
    ending_scale_factors,
    lexicon_matrix,
    sampling_warmth,
    sampling_noise,
):
    shards = lax.axis_size("tp")
    sections = lax.axis_size("section")
    rows, width = incoming_hidden_states.shape
    share = address_content_matrix.shape[2] // shards
    terms_shape = (sections * shards, rows // sections, width // shards)

    def exchange(terms, own, source):
        terms = lax.all_to_all(terms, ("section", "tp"), 0, 0)
        terms = terms[source * shards : (source + 1) * shards]
        block = (own + jnp.sum(terms.astype(jnp.float32), axis=0)).astype(jnp.bfloat16)
        copies = jnp.broadcast_to(block, terms_shape)
        return lax.all_to_all(copies, ("section", "tp"), 0, 0)

    terms, first, own, *held = first_layer(
        terms_shape,
        parent_positions,
        filled_extents,
        incoming_hidden_states,
        layer_scale_factors,
        question_matrix,
        address_content_matrix,
        projection_back_matrix,
        stored_address_tensor,
        stored_content_tensor,
    )
    blocks = exchange(terms, own, 0)
    terms, entry, own, warmth = next_layer(
        blocks,
        first,
        held,
        sampling_warmth,
        share,
    )
    blocks = exchange(terms, own, 1)
    stats, final_rows = local_stats(
        blocks,
        ending_scale_factors.reshape(width // HEAD, HEAD),
        warmth,
        sampling_noise,
        lexicon_matrix,
    )
    stats = lax.all_to_all(stats, ("section", "tp"), 0, 0)
    best_score, log_norm = combine(stats, rows)
    return (entry[None], final_rows, best_score, log_norm)


def solution(mesh):
    in_specs = (
        P(),
        P(),
        P(),
        P("section", None, None, None),
        P("section", None, None, None),
        P("section", None),
        P("section", None, "tp"),
        P("section", None, None),
        P("section", "tp", None),
        P(),
        P(("section", "tp"), None),
        P(),
        P(None, ("section", "tp")),
    )
    out_specs = (P("section", None, "tp"), P(), P(), P())
    return jax.shard_map(
        per_device, mesh=mesh, in_specs=in_specs, out_specs=out_specs, check_vma=False
    )
```

profile of v0, /device:TPU:1, one launch (start us, length us, event | category | flops | bytes accessed | tf_op | source)
XLA Modules:
  0.0 90.4 jit_solution(15794142643134093602)
XLA Ops:
  0.6 4.6 %first_layer.1 = (bf16[128,8,128]{2,1,0:T(8,128)(2,1)S(1)}, bf16[16,256]{1,0:T(8,128)(2,1)S(1)}, f32[8,128]{1,0:T(8,128)S(1)}, bf16[1,8192]{1,0:T(2,128)(2,1)S(1...) custom-call(s32[16]{0:T(128)} %parents_hbm.1, ...), custom_call_target="tpu_custom_call" | custom-call | tf_op jit(solution)/shard_map/first_layer/pallas_call | solution.py:253
  5.3 22.2 %all_to_all.25 = bf16[128,8,128]{2,1,0:T(8,128)(2,1)S(1)} all-to-all(bf16[128,8,128]{2,1,0:T(8,128)(2,1)S(1)} %get-tuple-element.23), channel_id=1, replica_groups=mesh['section'=2,'tp'=64] {'section','tp'}, dimensions={0} | all-to-all | bytes 524288 | tf_op jit(solution)/shard_map/all_to_all | solution.py:411
  27.5 0.1 convert_reduce_fusion.1
  27.6 14.7 %all_to_all.26.blocks_ref = bf16[128,8,128]{2,1,0:T(8,128)(2,1)S(1)} all-to-all(bf16[128,8,128]{2,1,0:T(8,128)(2,1)S(1)} %broadcast_in_dim.9), channel_id=1, replica_groups=mesh['section'=2,'tp'=64] {'section','tp'}, dimensions={0} | all-to-all | bytes 524288 | tf_op jit(solution)/shard_map/all_to_all | solution.py:415
  42.3 0.0 copy-start
  42.4 0.0 copy-start.1
  42.4 0.0 copy-start.2
  42.4 2.5 %next_layer.1 = (bf16[128,8,128]{2,1,0:T(8,128)(2,1)S(1)}, bf16[16,32]{1,0:T(8,128)(2,1)}, f32[8,128]{1,0:T(8,128)S(1)}, f32[16,128]{1,0:T(8,128)S(1)}) custom-call(bf16[128,8,128]{2,1,0:T(8,128)(2,1)S(1)} %all_to_all.26.blocks_ref, bf16[16,256]{1,0:T(8,128)(2,1)S(1)} %get-tuple-element.24.first_ref, bf16[1,8192]{1,0:T(2,128)(2,1)S(1)} %get-tuple-element.25.gain_ref, ...), custom_call_target="tpu_custom_call" | custom-call | tf_op jit(solution)/shard_map/next_layer/pallas_call | solution.py:287
  44.9 14.7 %all_to_all.27 = bf16[128,8,128]{2,1,0:T(8,128)(2,1)S(1)} all-to-all(bf16[128,8,128]{2,1,0:T(8,128)(2,1)S(1)} %get-tuple-element.34), channel_id=1, replica_groups=mesh['section'=2,'tp'=64] {'section','tp'}, dimensions={0} | all-to-all | bytes 524288 | tf_op jit(solution)/shard_map/all_to_all | solution.py:411
  59.6 0.1 convert_reduce_fusion
  59.7 14.7 %all_to_all.28.blocks_ref = bf16[128,8,128]{2,1,0:T(8,128)(2,1)S(1)} all-to-all(bf16[128,8,128]{2,1,0:T(8,128)(2,1)S(1)} %broadcast_in_dim.11), channel_id=1, replica_groups=mesh['section'=2,'tp'=64] {'section','tp'}, dimensions={0} | all-to-all | bytes 524288 | tf_op jit(solution)/shard_map/all_to_all | solution.py:415
  74.5 0.0 copy-done
  74.5 0.0 copy-done.1
  74.5 0.0 copy-done.2
  74.5 1.7 %local_stats.1 = (f32[128,1,128]{2,1,0:T(1,128)S(1)}, bf16[16,8192]{1,0:T(8,128)(2,1)}) custom-call(bf16[128,8,128]{2,1,0:T(8,128)(2,1)S(1)} %all_to_all.28.blocks_ref, bf16[64,128]{1,0:T(8,128)(2,1)S(1)} %bitcast.2, f32[16,128]{1,0:T(8,128)S(1)} %get-tuple-element.35.warmth_ref, f32[16,256]{1,0:T(8,128)S(1)} %copy-done.2, bf16[256,8192]{1,0:T(8,128)(2,1)S(1)} %copy-done), custom_call_target="tpu_custom_call" | custom-call | tf_op jit(solution)/shard_map/local_stats/pallas_call | solution.py:341
  76.2 13.3 %all_to_all.29.stats_ref = f32[128,1,128]{2,1,0:T(1,128)S(1)} all-to-all(f32[128,1,128]{2,1,0:T(1,128)S(1)} %get-tuple-element.37), channel_id=1, replica_groups=mesh['section'=2,'tp'=64] {'section','tp'}, dimensions={0} | all-to-all | bytes 131072 | tf_op jit(solution)/shard_map/all_to_all | solution.py:445
  89.6 0.8 combine.1
  (4 shorter events, 0.1 us)
Async XLA Ops:
  42.3 32.1 %copy-start = (bf16[256,8192]{1,0:T(8,128)(2,1)S(1)}, bf16[256,8192]{1,0:T(8,128)(2,1)}, u32[]{:S(2)}) copy-start(bf16[256,8192]{1,0:T(8,128)(2,1)} %lexicon_ref.1) | copy-start | bytes 12582916
  42.4 32.1 %copy-start.1 = (bf16[8192]{0:T(1024)(128)(2,1)S(1)}, bf16[8192]{0:T(1024)(128)(2,1)}, u32[]{:S(2)}) copy-start(bf16[8192]{0:T(1024)(128)(2,1)} %param.22) | copy-start | bytes 49156
  42.4 32.1 %copy-start.2 = (f32[16,256]{1,0:T(8,128)S(1)}, f32[16,256]{1,0:T(8,128)}, u32[]{:S(2)}) copy-start(f32[16,256]{1,0:T(8,128)} %noise_ref.1) | copy-start | bytes 49156
where the time goes:
time: 90.6 us; the launch traced here: 90.4 us
  blocking collectives  79.8 us (88%)
  Pallas kernels  9.68 us (11%)
    all_to_all x2, blocking collectives, exchange(): terms = lax.all_to_all(terms, ('section', 'tp'), 0, 0)  37 us
    all_to_all x2, blocking collectives, exchange(): return lax.all_to_all(copies, ('section', 'tp'), 0, 0)  29.5 us
    all_to_all x1, blocking collectives, per_device(): stats = lax.all_to_all(stats, ('section', 'tp'), 0, 0)  13.3 us
    pallas_call x1, Pallas kernels, first_layer(): pl.pallas_call(first_layer_kernel, out_shape=(bf16(terms_shape), bf16((ro...  4.64 us
    pallas_call x1, Pallas kernels, next_layer(): pl.pallas_call(next_layer_kernel, out_shape=(bf16(blocks.shape), bf16((ro...  2.52 us

commit v1 on v0

--- a/solution.py
+++ b/solution.py
@@ -91,6 +91,7 @@
 def first_layer_kernel(
     parents_hbm,
     extents_hbm,
+    warmth_hbm,
     hidden_hbm,
     gain_hbm,
     question_hbm,
@@ -108,8 +109,10 @@
     keys_ref,
     values_ref,
     visible_ref,
+    warmth_ref,
     parents,
     extents,
+    warmth,
     hidden_ref,
     address_ref,
     content_ref,
@@ -128,6 +131,7 @@
         pltpu.make_async_copy(gain_hbm, gain_ref, sems.at[1]),
         pltpu.make_async_copy(parents_hbm, parents, sems.at[4]),
         pltpu.make_async_copy(extents_hbm, extents, sems.at[5]),
+        pltpu.make_async_copy(warmth_hbm, warmth, sems.at[7]),
     ]
     lines = [
         pltpu.make_async_copy(address_hbm.at[0, :, :, head_columns], address_ref, sems.at[2]),
@@ -168,6 +172,7 @@
         if i == STEPS // 2:
             visible = column_of([extents[parents[j]] for j in range(rows)], rows)
             visible_ref[...] = visible
+            warmth_ref[...] = column_of([warmth[j] for j in range(rows)], rows)
             for copy in lines:
                 copy.wait()
             for j in range(rows):
@@ -198,17 +203,12 @@
     keys_ref,
     values_ref,
     visible_ref,
-    warmth_hbm,
     terms_ref,
     entry_hbm,
     own_ref,
-    warmth_ref,
     entry_ref,
-    warmth,
-    sems,
+    sem,
 ):
-    fetch = pltpu.make_async_copy(warmth_hbm, warmth, sems.at[0])
-    fetch.start()
     width = question_ref.shape[0]
     shards = lax.axis_size("tp")
     shard = lax.axis_index("tp")
@@ -217,21 +217,17 @@
     hidden = jnp.concatenate([whole_rows(blocks_ref, shards, k) for k in range(shards)], axis=1)
     squares = lane_squares(hidden)
     scaled = (hidden * gain_ref[...].astype(jnp.float32)).astype(jnp.bfloat16)
-    query = dot(scaled, question_ref[...])
-    pair = dot(scaled, pair_ref[...])
     squares = jnp.sum(squares, axis=1, keepdims=True)
     inverse = lax.rsqrt(squares * (1.0 / width) + epsilon)
-    query = (query * inverse).astype(jnp.bfloat16)
-    pair = (pair * inverse).astype(jnp.bfloat16)
+    pair = (dot(scaled, pair_ref[...]) * inverse).astype(jnp.bfloat16)
     both = jnp.where(lax.axis_index("section") == 0, first_ref[...], pair).astype(jnp.float32)
     share = entry_ref.shape[1]
     offset = shard % (shards // KV_HEADS) * share
-    both = pltpu.roll(both, 2 * HEAD - offset, 1)
+    both = pltpu.roll(both, (2 * HEAD - offset) % (2 * HEAD), 1)
     entry_ref[...] = both[:, :share].astype(jnp.bfloat16)
-    leave = pltpu.make_async_copy(entry_ref, entry_hbm, sems.at[1])
+    leave = pltpu.make_async_copy(entry_ref, entry_hbm, sem)
     leave.start()
-    fetch.wait()
-    warmth_ref[...] = column_of([warmth[j] for j in range(rows)], rows)
+    query = (dot(scaled, question_ref[...]) * inverse).astype(jnp.bfloat16)
     mixed = attend(query, pair, keys_ref[...], values_ref[...], visible_ref[...])
     store_terms(mixed, back_ref[...], terms_ref)
     leave.wait()
@@ -246,7 +242,7 @@
     return [pl.BlockSpec(memory_space=spaces[kind]) for kind in kinds]
 
 
-def first_layer(terms_shape, parents, extents, hidden, gain, question, pair, back, address, content):
+def first_layer(terms_shape, parents, extents, warmth, hidden, gain, question, pair, back, address, content):
     rows, width = hidden.shape
     slots = address.shape[2]
     bf16 = functools.partial(jax.ShapeDtypeStruct, dtype=jnp.bfloat16)
@@ -263,26 +259,28 @@
             bf16((rows * slots, HEAD)),
             bf16((rows * slots, HEAD)),
             jax.ShapeDtypeStruct((rows, HEAD), jnp.int32),
+            jax.ShapeDtypeStruct((rows, HEAD), jnp.float32),
         ),
-        in_specs=specs("hhhhhhhhh"),
-        out_specs=specs("v" * 10),
+        in_specs=specs("h" * 10),
+        out_specs=specs("v" * 11),
         scratch_shapes=[
             pltpu.SMEM((rows,), jnp.int32),
             pltpu.SMEM((rows,), jnp.int32),
+            pltpu.SMEM((rows,), jnp.float32),
             pltpu.VMEM((rows, width), jnp.bfloat16),
             pltpu.VMEM((rows, slots, HEAD), jnp.bfloat16),
             pltpu.VMEM((rows, slots, HEAD), jnp.bfloat16),
-            pltpu.SemaphoreType.DMA((7,)),
+            pltpu.SemaphoreType.DMA((8,)),
             pltpu.SemaphoreType.DMA((STEPS,)),
             pltpu.SemaphoreType.DMA((STEPS,)),
         ],
         compiler_params=pltpu.CompilerParams(vmem_limit_bytes=LIMIT),
         name="first_layer",
-    )(*in_hbm(parents, extents, hidden, gain, question, pair, back, address, content))
-
-
-def next_layer(blocks, first, held, warmth, share):
-    rows = warmth.shape[0]
+    )(*in_hbm(parents, extents, warmth, hidden, gain, question, pair, back, address, content))
+
+
+def next_layer(blocks, first, held, share):
+    rows = first.shape[0]
     bf16 = functools.partial(jax.ShapeDtypeStruct, dtype=jnp.bfloat16)
     return pl.pallas_call(
         next_layer_kernel,
@@ -290,22 +288,25 @@
             bf16(blocks.shape),
             bf16((rows, share)),
             jax.ShapeDtypeStruct(blocks.shape[1:], jnp.float32),
-            jax.ShapeDtypeStruct((rows, HEAD), jnp.float32),
         ),
-        in_specs=specs("v" * (2 + len(held)) + "h"),
-        out_specs=specs("vhvv"),
-        scratch_shapes=[
-            pltpu.VMEM((rows, share), jnp.bfloat16),
-            pltpu.SMEM((rows,), jnp.float32),
-            pltpu.SemaphoreType.DMA((2,)),
-        ],
+        in_specs=specs("v" * (2 + len(held))),
+        out_specs=specs("vhv"),
+        scratch_shapes=[pltpu.VMEM((rows, share), jnp.bfloat16), pltpu.SemaphoreType.DMA],
         compiler_params=pltpu.CompilerParams(vmem_limit_bytes=LIMIT),
         name="next_layer",
-    )(blocks, first, *held, *in_hbm(warmth))
+    )(blocks, first, *held)
 
 
 def stats_kernel(
-    blocks_ref, gain_ref, warmth_ref, noise_ref, lexicon_ref, out_ref, final_hbm, final_ref, sem
+    blocks_ref,
+    gain_ref,
+    warmth_ref,
+    noise_ref,
+    lexicon_ref,
+    out_ref,
+    final_hbm,
+    final_ref,
+    sem,
 ):
     rows, width = final_ref.shape
     shards = width // HEAD
@@ -346,7 +347,10 @@
         ),
         in_specs=specs("vvvvv"),
         out_specs=tuple(specs("vh")),
-        scratch_shapes=[pltpu.VMEM((rows, width), jnp.bfloat16), pltpu.SemaphoreType.DMA],
+        scratch_shapes=[
+            pltpu.VMEM((rows, width), jnp.bfloat16),
+            pltpu.SemaphoreType.DMA,
+        ],
         compiler_params=pltpu.CompilerParams(vmem_limit_bytes=LIMIT),
         name="local_stats",
     )(blocks, gain, warmth, noise, lexicon)
@@ -414,10 +418,11 @@
         copies = jnp.broadcast_to(block, terms_shape)
         return lax.all_to_all(copies, ("section", "tp"), 0, 0)
 
-    terms, first, own, *held = first_layer(
+    terms, first, own, *held, warmth = first_layer(
         terms_shape,
         parent_positions,
         filled_extents,
+        sampling_warmth,
         incoming_hidden_states,
         layer_scale_factors,
         question_matrix,
@@ -427,13 +432,7 @@
         stored_content_tensor,
     )
     blocks = exchange(terms, own, 0)
-    terms, entry, own, warmth = next_layer(
-        blocks,
-        first,
-        held,
-        sampling_warmth,
-        share,
-    )
+    terms, entry, own = next_layer(blocks, first, held, share)
     blocks = exchange(terms, own, 1)
     stats, final_rows = local_stats(
         blocks,

time: 90.6 us -> 90.2 us (level)
  no operation moved by 1% of the time
where the time goes in v1:
time: 90.2 us; the launch traced here: 90 us
  blocking collectives  79.8 us (88%)
  Pallas kernels  9.28 us (10%)
    all_to_all x2, blocking collectives, exchange(): terms = lax.all_to_all(terms, ('section', 'tp'), 0, 0)  37 us
    all_to_all x2, blocking collectives, exchange(): return lax.all_to_all(copies, ('section', 'tp'), 0, 0)  29.5 us
    all_to_all x1, blocking collectives, per_device(): stats = lax.all_to_all(stats, ('section', 'tp'), 0, 0)  13.3 us
    pallas_call x1, Pallas kernels, first_layer(): pl.pallas_call(first_layer_kernel, out_shape=(bf16(terms_shape), bf16((ro...  4.58 us
    pallas_call x1, Pallas kernels, next_layer(): pl.pallas_call(next_layer_kernel, out_shape=(bf16(blocks.shape), bf16((ro...  2.17 us

profile of v1, /device:TPU:1, one launch (start us, length us, event | category | flops | bytes accessed | tf_op | source)
XLA Modules:
  0.0 90.0 jit_solution(1801285221415742897)
XLA Ops:
  0.6 4.6 %first_layer.1 = (bf16[128,8,128]{2,1,0:T(8,128)(2,1)S(1)}, bf16[16,256]{1,0:T(8,128)(2,1)S(1)}, f32[8,128]{1,0:T(8,128)S(1)}, bf16[1,8192]{1,0:T(2,128)(2,1)S(1...) custom-call(s32[16]{0:T(128)} %parents_hbm.1, ...), custom_call_target="tpu_custom_call" | custom-call | tf_op jit(solution)/shard_map/first_layer/pallas_call | solution.py:249
  5.2 22.2 %all_to_all.25 = bf16[128,8,128]{2,1,0:T(8,128)(2,1)S(1)} all-to-all(bf16[128,8,128]{2,1,0:T(8,128)(2,1)S(1)} %get-tuple-element.23), channel_id=1, replica_groups=mesh['section'=2,'tp'=64] {'section','tp'}, dimensions={0} | all-to-all | bytes 524288 | tf_op jit(solution)/shard_map/all_to_all | solution.py:415
  27.4 0.1 convert_reduce_fusion.1
  27.6 14.7 %all_to_all.26.blocks_ref = bf16[128,8,128]{2,1,0:T(8,128)(2,1)S(1)} all-to-all(bf16[128,8,128]{2,1,0:T(8,128)(2,1)S(1)} %broadcast_in_dim.9), channel_id=1, replica_groups=mesh['section'=2,'tp'=64] {'section','tp'}, dimensions={0} | all-to-all | bytes 524288 | tf_op jit(solution)/shard_map/all_to_all | solution.py:419
  42.3 0.0 copy-start
  42.3 0.0 copy-start.1
  42.3 0.0 copy-start.2
  42.3 2.2 %next_layer.1 = (bf16[128,8,128]{2,1,0:T(8,128)(2,1)S(1)}, bf16[16,32]{1,0:T(8,128)(2,1)}, f32[8,128]{1,0:T(8,128)S(1)}) custom-call(bf16[128,8,128]{2,1,0:T(8,128)(2,1)S(1)} %all_to_all.26.blocks_ref, bf16[16,256]{1,0:T(8,128)(2,1)S(1)} %get-tuple-element.24.first_ref, bf16[1,8192]{1,0:T(2,128)(2,1)S(1)} %get-tuple-element.25.gain_ref, ...), custom_call_target="tpu_custom_call" | custom-call | tf_op jit(solution)/shard_map/next_layer/pallas_call | solution.py:285
  44.5 14.7 %all_to_all.27 = bf16[128,8,128]{2,1,0:T(8,128)(2,1)S(1)} all-to-all(bf16[128,8,128]{2,1,0:T(8,128)(2,1)S(1)} %get-tuple-element.34), channel_id=1, replica_groups=mesh['section'=2,'tp'=64] {'section','tp'}, dimensions={0} | all-to-all | bytes 524288 | tf_op jit(solution)/shard_map/all_to_all | solution.py:415
  59.2 0.1 convert_reduce_fusion
  59.3 14.7 %all_to_all.28.blocks_ref = bf16[128,8,128]{2,1,0:T(8,128)(2,1)S(1)} all-to-all(bf16[128,8,128]{2,1,0:T(8,128)(2,1)S(1)} %broadcast_in_dim.11), channel_id=1, replica_groups=mesh['section'=2,'tp'=64] {'section','tp'}, dimensions={0} | all-to-all | bytes 524288 | tf_op jit(solution)/shard_map/all_to_all | solution.py:419
  74.1 0.0 copy-done
  74.1 0.0 copy-done.1
  74.1 0.0 copy-done.2
  74.1 1.7 %local_stats.1 = (f32[128,1,128]{2,1,0:T(1,128)S(1)}, bf16[16,8192]{1,0:T(8,128)(2,1)}) custom-call(bf16[128,8,128]{2,1,0:T(8,128)(2,1)S(1)} %all_to_all.28.blocks_ref, bf16[64,128]{1,0:T(8,128)(2,1)S(1)} %bitcast.2, f32[16,128]{1,0:T(8,128)S(1)} %get-tuple-element.35.warmth_ref, f32[16,256]{1,0:T(8,128)S(1)} %copy-done.2, bf16[256,8192]{1,0:T(8,128)(2,1)S(1)} %copy-done), custom_call_target="tpu_custom_call" | custom-call | tf_op jit(solution)/shard_map/local_stats/pallas_call | solution.py:342
  75.8 13.3 %all_to_all.29.stats_ref = f32[128,1,128]{2,1,0:T(1,128)S(1)} all-to-all(f32[128,1,128]{2,1,0:T(1,128)S(1)} %get-tuple-element.37), channel_id=1, replica_groups=mesh['section'=2,'tp'=64] {'section','tp'}, dimensions={0} | all-to-all | bytes 131072 | tf_op jit(solution)/shard_map/all_to_all | solution.py:444
  89.2 0.8 combine.1
  (4 shorter events, 0.1 us)
Async XLA Ops:
  42.3 31.8 %copy-start = (bf16[256,8192]{1,0:T(8,128)(2,1)S(1)}, bf16[256,8192]{1,0:T(8,128)(2,1)}, u32[]{:S(2)}) copy-start(bf16[256,8192]{1,0:T(8,128)(2,1)} %lexicon_ref.1) | copy-start | bytes 12582916
  42.3 31.8 %copy-start.1 = (bf16[8192]{0:T(1024)(128)(2,1)S(1)}, bf16[8192]{0:T(1024)(128)(2,1)}, u32[]{:S(2)}) copy-start(bf16[8192]{0:T(1024)(128)(2,1)} %param.22) | copy-start | bytes 49156
  42.3 31.8 %copy-start.2 = (f32[16,256]{1,0:T(8,128)S(1)}, f32[16,256]{1,0:T(8,128)}, u32[]{:S(2)}) copy-start(f32[16,256]{1,0:T(8,128)} %noise_ref.1) | copy-start | bytes 49156

commit v2 on v1

--- a/solution.py
+++ b/solution.py
@@ -297,17 +297,7 @@
     )(blocks, first, *held)
 
 
-def stats_kernel(
-    blocks_ref,
-    gain_ref,
-    warmth_ref,
-    noise_ref,
-    lexicon_ref,
-    out_ref,
-    final_hbm,
-    final_ref,
-    sem,
-):
+def stats_kernel(blocks_ref, gain_ref, warmth_ref, noise_ref, lexicon_ref, out_ref, final_ref):
     rows, width = final_ref.shape
     shards = width // HEAD
     squares = jnp.zeros((rows, HEAD), jnp.float32)
@@ -317,8 +307,6 @@
         final_ref[:, k * HEAD : (k + 1) * HEAD] = hidden.astype(jnp.bfloat16)
         squares = squares + hidden * hidden
         pieces.append((hidden * gain_ref[k : k + 1].astype(jnp.float32)).astype(jnp.bfloat16))
-    leave = pltpu.make_async_copy(final_ref, final_hbm, sem)
-    leave.start()
     logits = dot(jnp.concatenate(pieces, axis=1), lexicon_ref[...], ((1,), (1,)))
     squares = jnp.sum(squares, axis=1, keepdims=True)
     inverse = lax.rsqrt(squares * (1.0 / width) + epsilon)
@@ -333,7 +321,6 @@
     packed = jnp.where(lane == row + rows, norm, packed)
     packed = jnp.sum(packed, axis=0, keepdims=True)
     out_ref[...] = jnp.broadcast_to(packed[None], out_ref.shape)
-    leave.wait()
 
 
 def local_stats(blocks, gain, warmth, noise, lexicon):
@@ -343,20 +330,20 @@
         stats_kernel,
         out_shape=(
             jax.ShapeDtypeStruct((blocks.shape[0], 1, HEAD), jnp.float32),
-            jax.ShapeDtypeStruct((rows, width), jnp.bfloat16),
+            pltpu.VMEM((rows, width), jnp.bfloat16),
         ),
         in_specs=specs("vvvvv"),
-        out_specs=tuple(specs("vh")),
-        scratch_shapes=[
-            pltpu.VMEM((rows, width), jnp.bfloat16),
-            pltpu.SemaphoreType.DMA,
-        ],
+        out_specs=tuple(specs("vv")),
         compiler_params=pltpu.CompilerParams(vmem_limit_bytes=LIMIT),
         name="local_stats",
     )(blocks, gain, warmth, noise, lexicon)
 
 
-def combine_kernel(stats_ref, best_hbm, norm_hbm, best_ref, norm_ref, sems):
+def combine_kernel(
+    stats_ref, final_ref, best_hbm, norm_hbm, final_hbm, best_ref, norm_ref, sems
+):
+    leave = pltpu.make_async_copy(final_ref, final_hbm, sems.at[2])
+    leave.start()
     rows = best_ref.shape[0]
     stats = stats_ref[...]
     highest = jnp.max(stats, axis=0)
@@ -371,23 +358,25 @@
         copy.start()
     for copy in copies:
         copy.wait()
-
-
-def combine(stats, rows):
+    leave.wait()
+
+
+def combine(stats, final):
+    rows = final.shape[0]
     row = jax.ShapeDtypeStruct((rows,), jnp.float32)
     return pl.pallas_call(
         combine_kernel,
-        out_shape=(row, row),
-        in_specs=specs("v"),
-        out_specs=specs("hh"),
-        compiler_params=pltpu.CompilerParams(vmem_limit_bytes=LIMIT // 4),
+        out_shape=(row, row, jax.ShapeDtypeStruct(final.shape, final.dtype)),
+        in_specs=specs("vv"),
+        out_specs=specs("hhh"),
         scratch_shapes=[
             pltpu.VMEM((rows,), jnp.float32),
             pltpu.VMEM((rows,), jnp.float32),
-            pltpu.SemaphoreType.DMA((2,)),
+            pltpu.SemaphoreType.DMA((3,)),
         ],
+        compiler_params=pltpu.CompilerParams(vmem_limit_bytes=LIMIT // 4),
         name="combine",
-    )(stats)
+    )(stats, pltpu.with_memory_space_constraint(final, pltpu.VMEM))
 
 
 def per_device(
@@ -442,7 +431,7 @@
         lexicon_matrix,
     )
     stats = lax.all_to_all(stats, ("section", "tp"), 0, 0)
-    best_score, log_norm = combine(stats, rows)
+    best_score, log_norm, final_rows = combine(stats, final_rows)
     return (entry[None], final_rows, best_score, log_norm)
 
 

time: 90.2 us -> 89.9 us (level)
  no operation moved by 1% of the time
where the time goes in v2:
time: 89.9 us; the launch traced here: 89.7 us
  blocking collectives  79.8 us (89%)
  Pallas kernels  8.98 us (10%)
    all_to_all x2, blocking collectives, exchange(): terms = lax.all_to_all(terms, ('section', 'tp'), 0, 0)  37 us
    all_to_all x2, blocking collectives, exchange(): return lax.all_to_all(copies, ('section', 'tp'), 0, 0)  29.5 us
    all_to_all x1, blocking collectives, per_device(): stats = lax.all_to_all(stats, ('section', 'tp'), 0, 0)  13.3 us
    pallas_call x1, Pallas kernels, first_layer(): pl.pallas_call(first_layer_kernel, out_shape=(bf16(terms_shape), bf16((ro...  4.58 us
    pallas_call x1, Pallas kernels, next_layer(): pl.pallas_call(next_layer_kernel, out_shape=(bf16(blocks.shape), bf16((ro...  2.17 us

profile of v2, /device:TPU:1, one launch (start us, length us, event | category | flops | bytes accessed | tf_op | source)
XLA Modules:
  0.0 89.7 jit_solution(76381571929989896)
XLA Ops:
  0.6 4.6 %first_layer.1 = (bf16[128,8,128]{2,1,0:T(8,128)(2,1)S(1)}, bf16[16,256]{1,0:T(8,128)(2,1)S(1)}, f32[8,128]{1,0:T(8,128)S(1)}, bf16[1,8192]{1,0:T(2,128)(2,1)S(1...) custom-call(s32[16]{0:T(128)} %parents_hbm.1, ...), custom_call_target="tpu_custom_call" | custom-call | tf_op jit(solution)/shard_map/first_layer/pallas_call | solution.py:249
  5.2 22.2 %all_to_all.25 = bf16[128,8,128]{2,1,0:T(8,128)(2,1)S(1)} all-to-all(bf16[128,8,128]{2,1,0:T(8,128)(2,1)S(1)} %get-tuple-element.24), channel_id=1, replica_groups=mesh['section'=2,'tp'=64] {'section','tp'}, dimensions={0} | all-to-all | bytes 524288 | tf_op jit(solution)/shard_map/all_to_all | solution.py:404
  27.4 0.1 convert_reduce_fusion.1
  27.6 14.7 %all_to_all.26.blocks_ref = bf16[128,8,128]{2,1,0:T(8,128)(2,1)S(1)} all-to-all(bf16[128,8,128]{2,1,0:T(8,128)(2,1)S(1)} %broadcast_in_dim.9), channel_id=1, replica_groups=mesh['section'=2,'tp'=64] {'section','tp'}, dimensions={0} | all-to-all | bytes 524288 | tf_op jit(solution)/shard_map/all_to_all | solution.py:408
  42.3 0.0 copy-start
  42.3 0.0 copy-start.1
  42.3 0.0 copy-start.2
  42.3 2.2 %next_layer.1 = (bf16[128,8,128]{2,1,0:T(8,128)(2,1)S(1)}, bf16[16,32]{1,0:T(8,128)(2,1)}, f32[8,128]{1,0:T(8,128)S(1)}) custom-call(bf16[128,8,128]{2,1,0:T(8,128)(2,1)S(1)} %all_to_all.26.blocks_ref, bf16[16,256]{1,0:T(8,128)(2,1)S(1)} %get-tuple-element.25.first_ref, bf16[1,8192]{1,0:T(2,128)(2,1)S(1)} %get-tuple-element.26.gain_ref, ...), custom_call_target="tpu_custom_call" | custom-call | tf_op jit(solution)/shard_map/next_layer/pallas_call | solution.py:285
  44.5 14.7 %all_to_all.27 = bf16[128,8,128]{2,1,0:T(8,128)(2,1)S(1)} all-to-all(bf16[128,8,128]{2,1,0:T(8,128)(2,1)S(1)} %get-tuple-element.35), channel_id=1, replica_groups=mesh['section'=2,'tp'=64] {'section','tp'}, dimensions={0} | all-to-all | bytes 524288 | tf_op jit(solution)/shard_map/all_to_all | solution.py:404
  59.2 0.1 convert_reduce_fusion
  59.3 14.7 %all_to_all.28.blocks_ref = bf16[128,8,128]{2,1,0:T(8,128)(2,1)S(1)} all-to-all(bf16[128,8,128]{2,1,0:T(8,128)(2,1)S(1)} %broadcast_in_dim.11), channel_id=1, replica_groups=mesh['section'=2,'tp'=64] {'section','tp'}, dimensions={0} | all-to-all | bytes 524288 | tf_op jit(solution)/shard_map/all_to_all | solution.py:408
  74.1 0.0 copy-done
  74.1 0.0 copy-done.1
  74.1 0.0 copy-done.2
  74.1 1.4 %local_stats.1 = (f32[128,1,128]{2,1,0:T(1,128)S(1)}, bf16[16,8192]{1,0:T(8,128)(2,1)S(1)}) custom-call(bf16[128,8,128]{2,1,0:T(8,128)(2,1)S(1)} %all_to_all.28.blocks_ref, bf16[64,128]{1,0:T(8,128)(2,1)S(1)} %bitcast.2, f32[16,128]{1,0:T(8,128)S(1)} %get-tuple-element.36.warmth_ref, f32[16,256]{1,0:T(8,128)S(1)} %copy-done.2, bf16[256,8192]{1,0:T(8,128)(2,1)S(1)} %copy-done), custom_call_target="tpu_custom_call" | custom-call | tf_op jit(solution)/shard_map/local_stats/pallas_call | solution.py:329
  75.5 13.3 %all_to_all.29.stats_ref = f32[128,1,128]{2,1,0:T(1,128)S(1)} all-to-all(f32[128,1,128]{2,1,0:T(1,128)S(1)} %get-tuple-element.37), channel_id=1, replica_groups=mesh['section'=2,'tp'=64] {'section','tp'}, dimensions={0} | all-to-all | bytes 131072 | tf_op jit(solution)/shard_map/all_to_all | solution.py:433
  88.9 0.8 combine.1
  (4 shorter events, 0.1 us)
Async XLA Ops:
  42.3 31.8 %copy-start = (bf16[256,8192]{1,0:T(8,128)(2,1)S(1)}, bf16[256,8192]{1,0:T(8,128)(2,1)}, u32[]{:S(2)}) copy-start(bf16[256,8192]{1,0:T(8,128)(2,1)} %lexicon_ref.1) | copy-start | bytes 12582916
  42.3 31.8 %copy-start.1 = (bf16[8192]{0:T(1024)(128)(2,1)S(1)}, bf16[8192]{0:T(1024)(128)(2,1)}, u32[]{:S(2)}) copy-start(bf16[8192]{0:T(1024)(128)(2,1)} %param.22) | copy-start | bytes 49156
  42.3 31.8 %copy-start.2 = (f32[16,256]{1,0:T(8,128)S(1)}, f32[16,256]{1,0:T(8,128)}, u32[]{:S(2)}) copy-start(f32[16,256]{1,0:T(8,128)} %noise_ref.1) | copy-start | bytes 49156

commit v3 on v2

--- a/solution.py
+++ b/solution.py
@@ -329,7 +329,7 @@
     return pl.pallas_call(
         stats_kernel,
         out_shape=(
-            jax.ShapeDtypeStruct((blocks.shape[0], 1, HEAD), jnp.float32),
+            jax.ShapeDtypeStruct((blocks.shape[0] // 8, 8, HEAD), jnp.float32),
             pltpu.VMEM((rows, width), jnp.bfloat16),
         ),
         in_specs=specs("vvvvv"),
@@ -346,8 +346,9 @@
     leave.start()
     rows = best_ref.shape[0]
     stats = stats_ref[...]
-    highest = jnp.max(stats, axis=0)
-    norm = highest + jnp.log(jnp.sum(jnp.exp(stats - highest[None]), axis=0))
+    highest = jnp.max(jnp.max(stats, axis=0), axis=0, keepdims=True)
+    mass = jnp.sum(jnp.exp(stats - highest[None]), axis=0)
+    norm = highest + jnp.log(jnp.sum(mass, axis=0, keepdims=True))
     best_ref[...] = highest[0, :rows]
     norm_ref[...] = norm[0, rows : 2 * rows]
     copies = [
@@ -430,7 +431,8 @@
         sampling_noise,
         lexicon_matrix,
     )
-    stats = lax.all_to_all(stats, ("section", "tp"), 0, 0)
+    stats = lax.all_to_all(stats.reshape(sections * shards, 1, HEAD), ("section", "tp"), 0, 0)
+    stats = stats.reshape(sections * shards // 8, 8, HEAD)
     best_score, log_norm, final_rows = combine(stats, final_rows)
     return (entry[None], final_rows, best_score, log_norm)
 

time: 89.9 us -> 89.8 us (level)
  no operation moved by 1% of the time
where the time goes in v3:
time: 89.8 us; the launch traced here: 89.6 us
  blocking collectives  79.8 us (89%)
  Pallas kernels  8.88 us (10%)
    all_to_all x2, blocking collectives, exchange(): terms = lax.all_to_all(terms, ('section', 'tp'), 0, 0)  37 us
    all_to_all x2, blocking collectives, exchange(): return lax.all_to_all(copies, ('section', 'tp'), 0, 0)  29.5 us
    all_to_all x1, blocking collectives, per_device(): lax.all_to_all(stats.reshape(sections * shards, 1, HEAD), ('section', 'tp...  13.3 us
    pallas_call x1, Pallas kernels, first_layer(): pl.pallas_call(first_layer_kernel, out_shape=(bf16(terms_shape), bf16((ro...  4.58 us
    pallas_call x1, Pallas kernels, next_layer(): pl.pallas_call(next_layer_kernel, out_shape=(bf16(blocks.shape), bf16((ro...  2.17 us

profile of v3, /device:TPU:1, one launch (start us, length us, event | category | flops | bytes accessed | tf_op | source)
XLA Modules:
  0.0 89.6 jit_solution(1855133436884592969)
XLA Ops:
  0.6 4.6 %first_layer.1 = (bf16[128,8,128]{2,1,0:T(8,128)(2,1)S(1)}, bf16[16,256]{1,0:T(8,128)(2,1)S(1)}, f32[8,128]{1,0:T(8,128)S(1)}, bf16[1,8192]{1,0:T(2,128)(2,1)S(1...) custom-call(s32[16]{0:T(128)} %parents_hbm.1, ...), custom_call_target="tpu_custom_call" | custom-call | tf_op jit(solution)/shard_map/first_layer/pallas_call | solution.py:249
  5.2 22.2 %all_to_all.25 = bf16[128,8,128]{2,1,0:T(8,128)(2,1)S(1)} all-to-all(bf16[128,8,128]{2,1,0:T(8,128)(2,1)S(1)} %get-tuple-element.24), channel_id=1, replica_groups=mesh['section'=2,'tp'=64] {'section','tp'}, dimensions={0} | all-to-all | bytes 524288 | tf_op jit(solution)/shard_map/all_to_all | solution.py:405
  27.4 0.1 convert_reduce_fusion.1
  27.6 14.7 %all_to_all.26.blocks_ref = bf16[128,8,128]{2,1,0:T(8,128)(2,1)S(1)} all-to-all(bf16[128,8,128]{2,1,0:T(8,128)(2,1)S(1)} %broadcast_in_dim.9), channel_id=1, replica_groups=mesh['section'=2,'tp'=64] {'section','tp'}, dimensions={0} | all-to-all | bytes 524288 | tf_op jit(solution)/shard_map/all_to_all | solution.py:409
  42.3 0.0 copy-start
  42.3 0.0 copy-start.1
  42.3 0.0 copy-start.2
  42.3 2.2 %next_layer.1 = (bf16[128,8,128]{2,1,0:T(8,128)(2,1)S(1)}, bf16[16,32]{1,0:T(8,128)(2,1)}, f32[8,128]{1,0:T(8,128)S(1)}) custom-call(bf16[128,8,128]{2,1,0:T(8,128)(2,1)S(1)} %all_to_all.26.blocks_ref, bf16[16,256]{1,0:T(8,128)(2,1)S(1)} %get-tuple-element.25.first_ref, bf16[1,8192]{1,0:T(2,128)(2,1)S(1)} %get-tuple-element.26.gain_ref, ...), custom_call_target="tpu_custom_call" | custom-call | tf_op jit(solution)/shard_map/next_layer/pallas_call | solution.py:285
  44.5 14.7 %all_to_all.27 = bf16[128,8,128]{2,1,0:T(8,128)(2,1)S(1)} all-to-all(bf16[128,8,128]{2,1,0:T(8,128)(2,1)S(1)} %get-tuple-element.35), channel_id=1, replica_groups=mesh['section'=2,'tp'=64] {'section','tp'}, dimensions={0} | all-to-all | bytes 524288 | tf_op jit(solution)/shard_map/all_to_all | solution.py:405
  59.2 0.1 convert_reduce_fusion
  59.3 14.7 %all_to_all.28.blocks_ref = bf16[128,8,128]{2,1,0:T(8,128)(2,1)S(1)} all-to-all(bf16[128,8,128]{2,1,0:T(8,128)(2,1)S(1)} %broadcast_in_dim.11), channel_id=1, replica_groups=mesh['section'=2,'tp'=64] {'section','tp'}, dimensions={0} | all-to-all | bytes 524288 | tf_op jit(solution)/shard_map/all_to_all | solution.py:409
  74.1 0.0 copy-done
  74.1 0.0 copy-done.1
  74.1 0.0 copy-done.2
  74.1 1.4 %local_stats.1 = (f32[16,8,128]{2,1,0:T(8,128)S(1)}, bf16[16,8192]{1,0:T(8,128)(2,1)S(1)}) custom-call(bf16[128,8,128]{2,1,0:T(8,128)(2,1)S(1)} %all_to_all.28.blocks_ref, bf16[64,128]{1,0:T(8,128)(2,1)S(1)} %bitcast.8, f32[16,128]{1,0:T(8,128)S(1)} %get-tuple-element.36.warmth_ref, f32[16,256]{1,0:T(8,128)S(1)} %copy-done.2, bf16[256,8192]{1,0:T(8,128)(2,1)S(1)} %copy-done), custom_call_target="tpu_custom_call" | custom-call | tf_op jit(solution)/shard_map/local_stats/pallas_call | solution.py:329
  75.5 13.3 %all_to_all.29 = f32[128,1,128]{2,1,0:T(1,128)S(1)} all-to-all(f32[128,1,128]{2,1,0:T(1,128)S(1)} %bitcast.7), channel_id=1, replica_groups=mesh['section'=2,'tp'=64] {'section','tp'}, dimensions={0} | all-to-all | bytes 131072 | tf_op jit(solution)/shard_map/all_to_all | solution.py:434
  88.8 0.7 combine.1
  (4 shorter events, 0.1 us)
Async XLA Ops:
  42.3 31.8 %copy-start = (bf16[256,8192]{1,0:T(8,128)(2,1)S(1)}, bf16[256,8192]{1,0:T(8,128)(2,1)}, u32[]{:S(2)}) copy-start(bf16[256,8192]{1,0:T(8,128)(2,1)} %lexicon_ref.1) | copy-start | bytes 12582916
  42.3 31.8 %copy-start.1 = (bf16[8192]{0:T(1024)(128)(2,1)S(1)}, bf16[8192]{0:T(1024)(128)(2,1)}, u32[]{:S(2)}) copy-start(bf16[8192]{0:T(1024)(128)(2,1)} %param.22) | copy-start | bytes 49156
  42.3 31.8 %copy-start.2 = (f32[16,256]{1,0:T(8,128)S(1)}, f32[16,256]{1,0:T(8,128)}, u32[]{:S(2)}) copy-start(f32[16,256]{1,0:T(8,128)} %noise_ref.1) | copy-start | bytes 49156

commit v4 on v3

--- a/solution.py
+++ b/solution.py
@@ -33,16 +33,18 @@
     return column
 
 
-def attend(query, pair, keys, values, visible_slots):
-    rows = query.shape[0]
-    slots = keys.shape[0] // rows
+def mask_of(visible_slots, rows, slots):
+    row = lax.broadcasted_iota(jnp.int32, (rows, rows * slots), 0)
+    column = lax.broadcasted_iota(jnp.int32, (rows, rows * slots), 1)
+    slot = column - row * slots
+    return ((slot >= 0) & (slot < visible_slots[:, :1])).astype(jnp.int32)
+
+
+def attend(query, pair, keys, values, mask):
     new_key = pair[:, :HEAD].astype(jnp.float32)
     new_value = pair[:, HEAD:].astype(jnp.float32)
     score_scale = HEAD ** (-0.5)
-    row = lax.broadcasted_iota(jnp.int32, (rows, rows * slots), 0)
-    column = lax.broadcasted_iota(jnp.int32, (rows, rows * slots), 1)
-    slot = column - row * slots
-    visible = (slot >= 0) & (slot < visible_slots[:, :1])
+    visible = mask != 0
     scores = dot(query, keys, ((1,), (1,))) * score_scale
     own_score = jnp.sum(query.astype(jnp.float32) * new_key, axis=1, keepdims=True) * score_scale
     highest = jnp.maximum(
@@ -51,8 +53,9 @@
     spread = jnp.where(visible, jnp.exp(scores - highest), 0.0)
     own_weight = jnp.exp(own_score - highest)
     denominator = jnp.sum(spread, axis=1, keepdims=True) + own_weight
-    probabilities = (spread / denominator).astype(jnp.bfloat16)
-    own_prob = (own_weight / denominator).astype(jnp.bfloat16).astype(jnp.float32)
+    share = 1.0 / denominator
+    probabilities = (spread * share).astype(jnp.bfloat16)
+    own_prob = (own_weight * share).astype(jnp.bfloat16).astype(jnp.float32)
     mixed = dot(probabilities, values) + own_prob * new_value
     return mixed.astype(jnp.bfloat16)
 
@@ -170,7 +173,8 @@
         squares = squares + lane_squares(hidden)
         scaled = (hidden * gain_ref[:, part].astype(jnp.float32)).astype(jnp.bfloat16)
         if i == STEPS // 2:
-            visible = column_of([extents[parents[j]] for j in range(rows)], rows)
+            limits = column_of([extents[parents[j]] for j in range(rows)], rows)
+            visible = mask_of(limits, rows, slots)
             visible_ref[...] = visible
             warmth_ref[...] = column_of([warmth[j] for j in range(rows)], rows)
             for copy in lines:
@@ -258,7 +262,7 @@
             bf16((HEAD, width)),
             bf16((rows * slots, HEAD)),
             bf16((rows * slots, HEAD)),
-            jax.ShapeDtypeStruct((rows, HEAD), jnp.int32),
+            jax.ShapeDtypeStruct((rows, rows * slots), jnp.int32),
             jax.ShapeDtypeStruct((rows, HEAD), jnp.float32),
         ),
         in_specs=specs("h" * 10),

time: 89.8 us -> 89.7 us (level)
  no operation moved by 1% of the time
where the time goes in v4:
time: 89.7 us; the launch traced here: 89.5 us
  blocking collectives  79.8 us (89%)
  Pallas kernels  8.82 us (10%)
    all_to_all x2, blocking collectives, exchange(): terms = lax.all_to_all(terms, ('section', 'tp'), 0, 0)  36.9 us
    all_to_all x2, blocking collectives, exchange(): return lax.all_to_all(copies, ('section', 'tp'), 0, 0)  29.5 us
    all_to_all x1, blocking collectives, per_device(): lax.all_to_all(stats.reshape(sections * shards, 1, HEAD), ('section', 'tp...  13.3 us
    pallas_call x1, Pallas kernels, first_layer(): pl.pallas_call(first_layer_kernel, out_shape=(bf16(terms_shape), bf16((ro...  4.57 us
    pallas_call x1, Pallas kernels, next_layer(): pl.pallas_call(next_layer_kernel, out_shape=(bf16(blocks.shape), bf16((ro...  2.13 us

profile of v4, /device:TPU:1, one launch (start us, length us, event | category | flops | bytes accessed | tf_op | source)
XLA Modules:
  0.0 89.5 jit_solution(9774407421779263085)
XLA Ops:
  0.6 4.6 %first_layer.1 = (bf16[128,8,128]{2,1,0:T(8,128)(2,1)S(1)}, bf16[16,256]{1,0:T(8,128)(2,1)S(1)}, f32[8,128]{1,0:T(8,128)S(1)}, bf16[1,8192]{1,0:T(2,128)(2,1)S(1...) custom-call(s32[16]{0:T(128)} %parents_hbm.1, ...), custom_call_target="tpu_custom_call" | custom-call | tf_op jit(solution)/shard_map/first_layer/pallas_call | solution.py:253
  5.2 22.2 %all_to_all.25 = bf16[128,8,128]{2,1,0:T(8,128)(2,1)S(1)} all-to-all(bf16[128,8,128]{2,1,0:T(8,128)(2,1)S(1)} %get-tuple-element.24), channel_id=1, replica_groups=mesh['section'=2,'tp'=64] {'section','tp'}, dimensions={0} | all-to-all | bytes 524288 | tf_op jit(solution)/shard_map/all_to_all | solution.py:409
  27.4 0.1 convert_reduce_fusion.1
  27.5 14.7 %all_to_all.26.blocks_ref = bf16[128,8,128]{2,1,0:T(8,128)(2,1)S(1)} all-to-all(bf16[128,8,128]{2,1,0:T(8,128)(2,1)S(1)} %broadcast_in_dim.9), channel_id=1, replica_groups=mesh['section'=2,'tp'=64] {'section','tp'}, dimensions={0} | all-to-all | bytes 524288 | tf_op jit(solution)/shard_map/all_to_all | solution.py:413
  42.3 0.0 copy-start
  42.3 0.0 copy-start.1
  42.3 0.0 copy-start.2
  42.3 2.1 %next_layer.1 = (bf16[128,8,128]{2,1,0:T(8,128)(2,1)S(1)}, bf16[16,32]{1,0:T(8,128)(2,1)}, f32[8,128]{1,0:T(8,128)S(1)}) custom-call(bf16[128,8,128]{2,1,0:T(8,128)(2,1)S(1)} %all_to_all.26.blocks_ref, bf16[16,256]{1,0:T(8,128)(2,1)S(1)} %get-tuple-element.25.first_ref, bf16[1,8192]{1,0:T(2,128)(2,1)S(1)} %get-tuple-element.26.gain_ref, ...), custom_call_target="tpu_custom_call" | custom-call | tf_op jit(solution)/shard_map/next_layer/pallas_call | solution.py:289
  44.4 14.7 %all_to_all.27 = bf16[128,8,128]{2,1,0:T(8,128)(2,1)S(1)} all-to-all(bf16[128,8,128]{2,1,0:T(8,128)(2,1)S(1)} %get-tuple-element.35), channel_id=1, replica_groups=mesh['section'=2,'tp'=64] {'section','tp'}, dimensions={0} | all-to-all | bytes 524288 | tf_op jit(solution)/shard_map/all_to_all | solution.py:409
  59.2 0.1 convert_reduce_fusion
  59.3 14.7 %all_to_all.28.blocks_ref = bf16[128,8,128]{2,1,0:T(8,128)(2,1)S(1)} all-to-all(bf16[128,8,128]{2,1,0:T(8,128)(2,1)S(1)} %broadcast_in_dim.11), channel_id=1, replica_groups=mesh['section'=2,'tp'=64] {'section','tp'}, dimensions={0} | all-to-all | bytes 524288 | tf_op jit(solution)/shard_map/all_to_all | solution.py:413
  74.0 0.0 copy-done
  74.0 0.0 copy-done.1
  74.0 0.0 copy-done.2
  74.0 1.4 %local_stats.1 = (f32[16,8,128]{2,1,0:T(8,128)S(1)}, bf16[16,8192]{1,0:T(8,128)(2,1)S(1)}) custom-call(bf16[128,8,128]{2,1,0:T(8,128)(2,1)S(1)} %all_to_all.28.blocks_ref, bf16[64,128]{1,0:T(8,128)(2,1)S(1)} %bitcast.8, f32[16,128]{1,0:T(8,128)S(1)} %get-tuple-element.36.warmth_ref, f32[16,256]{1,0:T(8,128)S(1)} %copy-done.2, bf16[256,8192]{1,0:T(8,128)(2,1)S(1)} %copy-done), custom_call_target="tpu_custom_call" | custom-call | tf_op jit(solution)/shard_map/local_stats/pallas_call | solution.py:333
  75.4 13.3 %all_to_all.29 = f32[128,1,128]{2,1,0:T(1,128)S(1)} all-to-all(f32[128,1,128]{2,1,0:T(1,128)S(1)} %bitcast.7), channel_id=1, replica_groups=mesh['section'=2,'tp'=64] {'section','tp'}, dimensions={0} | all-to-all | bytes 131072 | tf_op jit(solution)/shard_map/all_to_all | solution.py:438
  88.8 0.7 combine.1
  (4 shorter events, 0.1 us)
Async XLA Ops:
  42.3 31.7 %copy-start = (bf16[256,8192]{1,0:T(8,128)(2,1)S(1)}, bf16[256,8192]{1,0:T(8,128)(2,1)}, u32[]{:S(2)}) copy-start(bf16[256,8192]{1,0:T(8,128)(2,1)} %lexicon_ref.1) | copy-start | bytes 12582916
  42.3 31.7 %copy-start.1 = (bf16[8192]{0:T(1024)(128)(2,1)S(1)}, bf16[8192]{0:T(1024)(128)(2,1)}, u32[]{:S(2)}) copy-start(bf16[8192]{0:T(1024)(128)(2,1)} %param.22) | copy-start | bytes 49156
  42.3 31.7 %copy-start.2 = (f32[16,256]{1,0:T(8,128)S(1)}, f32[16,256]{1,0:T(8,128)}, u32[]{:S(2)}) copy-start(f32[16,256]{1,0:T(8,128)} %noise_ref.1) | copy-start | bytes 49156
